TPU v7x, 32 devices: a whole 2x2x4 slice. The times are simulated.
32 devices in a mesh: groups: 2 (over y), ta: 16 (over z, x, core).
Axes of the slice: x: 2, y: 2, z: 4, core: 2. Of those that a mesh axis runs over, the one named last changes fastest.
Arguments:
- sources: float32 [32, 2, 2, 2, 2, 96, 128], P(('groups', 'ta')), parts along dimension 0, may hold values from -6 to 6
- coarse_blocks: bfloat16 [32, 2, 2, 2, 2, 9, 128, 128], P(('groups', 'ta')), parts along dimension 0, may hold values from -0.5 to 0.5
Outputs:
- solution: float32 [32, 2, 2, 2, 2, 96, 128], P(('groups', 'ta')), parts along dimension 0
- residual: float32 [32, 2, 2, 2, 2, 96, 128], P(('groups', 'ta')), parts along dimension 0
There are 2 independent parts, one for each index of `groups`. A program takes and returns all parts, laid end to end along the dimension named above; each array names one. Nothing has to cross between parts.
All inputs are finite; a program needn't handle non-finite values.
Results may differ from a plain program's by a relative error of at most 0.012.
Values may be sent and summed in bfloat16 or wider, within the bound.
A program may use at most 64 MiB of HBM per device.

v0:
```python
import jax
import jax.numpy as jnp
from jax import lax
from jax.sharding import PartitionSpec as P

CYCLES = 2
KRYLOV = 4


mass_term = 3.5


def passed_along(value, axis, steps):
    count = lax.axis_size(axis)
    pairs = [(source, (source + steps) % count) for source in range(count)]
    return lax.ppermute(value, axis, pairs)


def from_partner(block, axis, bit):
    count = lax.axis_size(axis)
    route = []
    for low in range(count):
        high = low | 1 << bit
        if high != low and high < count:
            route += [(low, high), (high, low)]
    return lax.ppermute(block, axis, route)


def edges(rounded, axis_index):
    length = rounded.shape[axis_index]
    first = lax.slice_in_dim(rounded, 0, 1, axis=axis_index)
    last = lax.slice_in_dim(rounded, length - 1, length, axis=axis_index)
    return jnp.stack([first, last])


def hops(rounded, axis_index, ahead, behind):
    length = rounded.shape[axis_index]
    forward = jnp.concatenate(
        [lax.slice_in_dim(rounded, 1, length, axis=axis_index), ahead], axis_index
    )
    backward = jnp.concatenate(
        [behind, lax.slice_in_dim(rounded, 0, length - 1, axis=axis_index)], axis_index
    )
    return (forward, backward)


def operate(field, blocks_here):
    rounded = field.astype(jnp.bfloat16)
    ahead_time = passed_along(rounded[:1], "ta", -8)
    behind_time = passed_along(rounded[-1:], "ta", 8)
    depth_faces = from_partner(edges(rounded, 1), "ta", 2)
    width_faces = from_partner(edges(rounded, 3), "ta", 0)
    height_faces = from_partner(edges(rounded, 2), "ta", 1)
    pair_width = hops(rounded, 3, width_faces[0], width_faces[1])
    pair_height = hops(rounded, 2, height_faces[0], height_faces[1])
    pair_depth = hops(rounded, 1, depth_faces[0], depth_faces[1])
    pair_time = hops(rounded, 0, ahead_time, behind_time)
    neighbours = [rounded]
    for pair in (pair_width, pair_height, pair_depth, pair_time):
        neighbours.append(-pair[0])
        neighbours.append(-pair[1])
    stacked = jnp.stack(neighbours, axis=4)
    shape = field.shape
    count = shape[0] * shape[1] * shape[2] * shape[3]
    flat_stack = stacked.reshape(count, 9, shape[4], shape[5])
    flat_blocks = blocks_here.reshape(count, 9, shape[5], shape[5])
    product = jnp.einsum(
        "skri,skoi->sro", flat_stack, flat_blocks, preferred_element_type=jnp.float32
    )
    return mass_term * field + product.reshape(shape)


def dot_fields(first, second):
    return jnp.sum(first * second, axis=(0, 1, 2, 3, 5))


def solve(sources, blocks_here):
    solution = jnp.zeros_like(sources)
    residual = sources
    for restart in range(CYCLES):
        directions = []
        images = []
        image_norms = []
        for step_index in range(KRYLOV):
            direction = residual
            image = operate(direction, blocks_here)
            if step_index > 0:
                local_heights = jnp.stack([dot_fields(earlier, image) for earlier in images])
                heights = lax.psum(local_heights, "ta")
                for earlier_index in range(step_index):
                    factor = (heights[earlier_index] / image_norms[earlier_index])[:, None]
                    image = image - factor * images[earlier_index]
                    direction = direction - factor * directions[earlier_index]
            norm_now, toward = lax.psum(
                (dot_fields(image, image), dot_fields(image, residual)), "ta"
            )
            alpha = (toward / norm_now)[:, None]
            solution = solution + alpha * direction
            residual = residual - alpha * image
            directions.append(direction)
            images.append(image)
            image_norms.append(norm_now)
    return (solution, residual)


def shards(sources, coarse_blocks):
    field = sources[0]
    blocks_here = coarse_blocks[0]
    solution, residual = solve(field, blocks_here)
    return (solution[None], residual[None])


def solution(mesh):
    placed = (
        P(("groups", "ta"), None, None, None, None, None, None),
        P(("groups", "ta"), None, None, None, None, None, None, None),
    )
    return jax.shard_map(
        shards,
        mesh=mesh,
        in_specs=placed,
        out_specs=(
            P(("groups", "ta"), None, None, None, None, None, None),
            P(("groups", "ta"), None, None, None, None, None, None),
        ),
        check_vma=False,
    )
```

profile of v0, /device:TPU:0, one launch (start us, length us, event | category | flops | bytes accessed | tf_op | source)
XLA Modules:
  0.0 676.4 jit_solution(10260077166984690391)
XLA Ops:
  10.6 8.2 %collective-permute-done.3 = bf16[1,2,2,2,96,128]{5,4,3,2,1,0:T(8,128)(2,1)S(1)} collective-permute-done((bf16[1,2,2,2,96,128]{5,4,3,2,1,0:T(8,128)(2,1)S(1)}, bf16[1,2,2,2,96,128]{5,4,3,2,1,0:T(8,128)(2,1)S(1)}, u32[]{:S(2)}, u32[]{:S(2)}) %collective-permute-start.3) | collective-permute-done | bytes 196640 | tf_op jit(solution)/shard_map/ppermute | solution.py:16
  18.9 6.8 %collective-permute-done.4 = bf16[1,2,2,2,96,128]{5,4,3,2,1,0:T(8,128)(2,1)S(1)} collective-permute-done((bf16[1,2,2,2,96,128]{5,4,3,2,1,0:T(8,128)(2,1)S(1)}, bf16[1,2,2,2,96,128]{5,4,3,2,1,0:T(8,128)(2,1)S(1)}, u32[]{:S(2)}, u32[]{:S(2)}) %collective-permute-start.4) | collective-permute-done | bytes 196640 | tf_op jit(solution)/shard_map/ppermute | solution.py:16
  30.8 30.3 %all-reduce.7 = (f32[96]{0:T(128)S(1)}, f32[96]{0:T(128)S(1)}) all-reduce(f32[96]{0:T(128)S(1)} %fusion.16, f32[96]{0:T(128)S(1)} %get-tuple-element.64), channel_id=1, replica_groups=mesh['groups'=2,'ta'=16] {'ta'}, use_global_device_ids=true, to_apply=%region_1.0 | all-reduce | flops 192 | bytes 1536 | tf_op jit(solution)/shard_map/psum | solution.py:94
  62.5 3.0 collective-permute-start.9
  65.6 8.8 %collective-permute-done.8 = bf16[1,2,2,2,96,128]{5,4,3,2,1,0:T(8,128)(2,1)S(1)} collective-permute-done((bf16[1,2,2,2,96,128]{5,4,3,2,1,0:T(8,128)(2,1)S(1)}, bf16[1,2,2,2,96,128]{5,4,3,2,1,0:T(8,128)(2,1)S(1)}, u32[]{:S(2)}, u32[]{:S(2)}) %collective-permute-start.8) | collective-permute-done | bytes 196640 | tf_op jit(solution)/shard_map/ppermute | solution.py:16
  74.5 4.1 collective-permute-done.9
  79.2 5.6 collective-permute-done.7
  87.8 29.5 %psum.156 = f32[96]{0:T(128)S(1)} all-reduce(f32[96]{0:T(128)S(1)} %get-tuple-element.257), channel_id=1, replica_groups=mesh['groups'=2,'ta'=16] {'ta'}, use_global_device_ids=true, to_apply=%region_5.0 | all-reduce | flops 96 | bytes 768 | tf_op jit(solution)/shard_map/psum | solution.py:89
  119.7 29.7 %all-reduce.6 = (f32[96]{0:T(128)S(1)}, f32[96]{0:T(128)S(1)}) all-reduce(f32[96]{0:T(128)S(1)} %get-tuple-element.25, f32[96]{0:T(128)S(1)} %get-tuple-element.24), channel_id=1, replica_groups=mesh['groups'=2,'ta'=16] {'ta'}, use_global_device_ids=true, to_apply=%region_7.0 | all-reduce | flops 192 | bytes 1536 | tf_op jit(solution)/shard_map/psum | solution.py:94
  151.3 3.0 collective-permute-start.14
  154.4 8.8 %collective-permute-done.13 = bf16[1,2,2,2,96,128]{5,4,3,2,1,0:T(8,128)(2,1)S(1)} collective-permute-done((bf16[1,2,2,2,96,128]{5,4,3,2,1,0:T(8,128)(2,1)S(1)}, bf16[1,2,2,2,96,128]{5,4,3,2,1,0:T(8,128)(2,1)S(1)}, u32[]{:S(2)}, u32[]{:S(2)}) %collective-permute-start.13) | collective-permute-done | bytes 196640 | tf_op jit(solution)/shard_map/ppermute | solution.py:16
  163.3 4.1 collective-permute-done.14
  168.0 5.6 collective-permute-done.12
  176.7 29.5 %psum.159 = f32[2,96]{1,0:T(2,128)S(1)} all-reduce(f32[2,96]{1,0:T(2,128)S(1)} %pad_maximum_fusion.26), channel_id=1, replica_groups=mesh['groups'=2,'ta'=16] {'ta'}, use_global_device_ids=true, to_apply=%region_12.0 | all-reduce | flops 192 | bytes 1536 | tf_op jit(solution)/shard_map/psum | solution.py:89
  208.9 29.5 %all-reduce.5 = (f32[96]{0:T(128)S(1)}, f32[96]{0:T(128)S(1)}) all-reduce(f32[96]{0:T(128)S(1)} %get-tuple-element.23, f32[96]{0:T(128)S(1)} %get-tuple-element.22), channel_id=1, replica_groups=mesh['groups'=2,'ta'=16] {'ta'}, use_global_device_ids=true, to_apply=%region_14.0 | all-reduce | flops 192 | bytes 1536 | tf_op jit(solution)/shard_map/psum | solution.py:94
  241.7 3.0 collective-permute-start.19
  244.8 8.8 %collective-permute-done.18 = bf16[1,2,2,2,96,128]{5,4,3,2,1,0:T(8,128)(2,1)S(1)} collective-permute-done((bf16[1,2,2,2,96,128]{5,4,3,2,1,0:T(8,128)(2,1)S(1)}, bf16[1,2,2,2,96,128]{5,4,3,2,1,0:T(8,128)(2,1)S(1)}, u32[]{:S(2)}, u32[]{:S(2)}) %collective-permute-start.18) | collective-permute-done | bytes 196640 | tf_op jit(solution)/shard_map/ppermute | solution.py:16
  253.7 4.1 collective-permute-done.19
  258.4 5.6 collective-permute-done.17
  265.5 3.1 multiply_reduce_fusion.18
  268.6 29.5 %psum.162 = f32[3,96]{1,0:T(4,128)S(1)} all-reduce(f32[3,96]{1,0:T(4,128)S(1)} %pad_maximum_fusion.24), channel_id=1, replica_groups=mesh['groups'=2,'ta'=16] {'ta'}, use_global_device_ids=true, to_apply=%region_20.0 | all-reduce | flops 288 | bytes 2304 | tf_op jit(solution)/shard_map/psum | solution.py:89
  298.1 3.4 multiply_reduce_fusion.14
  301.4 29.7 %all-reduce.4 = (f32[96]{0:T(128)S(1)}, f32[96]{0:T(128)S(1)}) all-reduce(f32[96]{0:T(128)S(1)} %get-tuple-element.18, f32[96]{0:T(128)S(1)} %get-tuple-element.17), channel_id=1, replica_groups=mesh['groups'=2,'ta'=16] {'ta'}, use_global_device_ids=true, to_apply=%region_22.0 | all-reduce | flops 192 | bytes 1536 | tf_op jit(solution)/shard_map/psum | solution.py:94
  331.1 3.4 fusion.22
  336.4 3.0 collective-permute-start.24
  339.5 8.8 %collective-permute-done.23 = bf16[1,2,2,2,96,128]{5,4,3,2,1,0:T(8,128)(2,1)S(1)} collective-permute-done((bf16[1,2,2,2,96,128]{5,4,3,2,1,0:T(8,128)(2,1)S(1)}, bf16[1,2,2,2,96,128]{5,4,3,2,1,0:T(8,128)(2,1)S(1)}, u32[]{:S(2)}, u32[]{:S(2)}) %collective-permute-start.23) | collective-permute-done | bytes 196640 | tf_op jit(solution)/shard_map/ppermute | solution.py:16
  348.4 4.1 collective-permute-done.24
  353.2 5.6 collective-permute-done.22
  362.6 29.5 %all-reduce.3 = (f32[96]{0:T(128)S(1)}, f32[96]{0:T(128)S(1)}) all-reduce(f32[96]{0:T(128)S(1)} %get-tuple-element.16, f32[96]{0:T(128)S(1)} %get-tuple-element.15), channel_id=1, replica_groups=mesh['groups'=2,'ta'=16] {'ta'}, use_global_device_ids=true, to_apply=%region_26.0 | all-reduce | flops 192 | bytes 1536 | tf_op jit(solution)/shard_map/psum | solution.py:94
  398.1 8.8 %collective-permute-done.28 = bf16[1,2,2,2,96,128]{5,4,3,2,1,0:T(8,128)(2,1)S(1)} collective-permute-done((bf16[1,2,2,2,96,128]{5,4,3,2,1,0:T(8,128)(2,1)S(1)}, bf16[1,2,2,2,96,128]{5,4,3,2,1,0:T(8,128)(2,1)S(1)}, u32[]{:S(2)}, u32[]{:S(2)}) %collective-permute-start.28) | collective-permute-done | bytes 196640 | tf_op jit(solution)/shard_map/ppermute | solution.py:16
  407.0 4.1 collective-permute-done.29
  411.7 5.6 collective-permute-done.27
  421.2 29.5 %psum.167 = f32[96]{0:T(128)S(1)} all-reduce(f32[96]{0:T(128)S(1)} %get-tuple-element.262), channel_id=1, replica_groups=mesh['groups'=2,'ta'=16] {'ta'}, use_global_device_ids=true, to_apply=%region_30.0 | all-reduce | flops 96 | bytes 768 | tf_op jit(solution)/shard_map/psum | solution.py:89
  453.3 29.7 %all-reduce.2 = (f32[96]{0:T(128)S(1)}, f32[96]{0:T(128)S(1)}) all-reduce(f32[96]{0:T(128)S(1)} %get-tuple-element.14, f32[96]{0:T(128)S(1)} %get-tuple-element.13), channel_id=1, replica_groups=mesh['groups'=2,'ta'=16] {'ta'}, use_global_device_ids=true, to_apply=%region_32.0 | all-reduce | flops 192 | bytes 1536 | tf_op jit(solution)/shard_map/psum | solution.py:94
  489.6 8.8 %collective-permute-done.33 = bf16[1,2,2,2,96,128]{5,4,3,2,1,0:T(8,128)(2,1)S(1)} collective-permute-done((bf16[1,2,2,2,96,128]{5,4,3,2,1,0:T(8,128)(2,1)S(1)}, bf16[1,2,2,2,96,128]{5,4,3,2,1,0:T(8,128)(2,1)S(1)}, u32[]{:S(2)}, u32[]{:S(2)}) %collective-permute-start.33) | collective-permute-done | bytes 196640 | tf_op jit(solution)/shard_map/ppermute | solution.py:16
  498.5 4.1 collective-permute-done.34
  503.3 5.6 collective-permute-done.32
  512.8 29.5 %psum.170 = f32[2,96]{1,0:T(2,128)S(1)} all-reduce(f32[2,96]{1,0:T(2,128)S(1)} %pad_maximum_fusion.27), channel_id=1, replica_groups=mesh['groups'=2,'ta'=16] {'ta'}, use_global_device_ids=true, to_apply=%region_37.0 | all-reduce | flops 192 | bytes 1536 | tf_op jit(solution)/shard_map/psum | solution.py:89
  542.3 3.0 multiply_reduce_fusion.6
  545.3 29.5 %all-reduce.1 = (f32[96]{0:T(128)S(1)}, f32[96]{0:T(128)S(1)}) all-reduce(f32[96]{0:T(128)S(1)} %get-tuple-element.12, f32[96]{0:T(128)S(1)} %get-tuple-element.11), channel_id=1, replica_groups=mesh['groups'=2,'ta'=16] {'ta'}, use_global_device_ids=true, to_apply=%region_41.0 | all-reduce | flops 192 | bytes 1536 | tf_op jit(solution)/shard_map/psum | solution.py:94
  581.9 8.8 %collective-permute-done.38 = bf16[1,2,2,2,96,128]{5,4,3,2,1,0:T(8,128)(2,1)S(1)} collective-permute-done((bf16[1,2,2,2,96,128]{5,4,3,2,1,0:T(8,128)(2,1)S(1)}, bf16[1,2,2,2,96,128]{5,4,3,2,1,0:T(8,128)(2,1)S(1)}, u32[]{:S(2)}, u32[]{:S(2)}) %collective-permute-start.38) | collective-permute-done | bytes 196640 | tf_op jit(solution)/shard_map/ppermute | solution.py:16
  590.8 4.1 collective-permute-done.39
  595.5 5.6 collective-permute-done.37
  602.6 3.0 multiply_reduce_fusion.4
  605.6 29.6 %psum.173 = f32[3,96]{1,0:T(4,128)S(1)} all-reduce(f32[3,96]{1,0:T(4,128)S(1)} %pad_maximum_fusion.25), channel_id=1, replica_groups=mesh['groups'=2,'ta'=16] {'ta'}, use_global_device_ids=true, to_apply=%region_45.0 | all-reduce | flops 288 | bytes 2304 | tf_op jit(solution)/shard_map/psum | solution.py:89
  638.0 29.8 %all-reduce = (f32[96]{0:T(128)S(1)}, f32[96]{0:T(128)S(1)}) all-reduce(f32[96]{0:T(128)S(1)} %get-tuple-element.7, f32[96]{0:T(128)S(1)} %get-tuple-element.6), channel_id=1, replica_groups=mesh['groups'=2,'ta'=16] {'ta'}, use_global_device_ids=true, to_apply=%region_47.0 | all-reduce | flops 192 | bytes 1536 | tf_op jit(solution)/shard_map/psum | solution.py:94
  667.9 4.8 multiply_add_fusion
  672.7 3.1 multiply_subtract_fusion
  (448 shorter events, 77.4 us)
Async XLA Ops:
  2.3 23.4 %collective-permute-start = (bf16[2,2,2,2,1,96,128]{6,5,3,2,1,4,0:T(8,128)(2,1)S(1)}, bf16[2,2,2,2,1,96,128]{6,5,3,2,1,4,0:T(8,128)(2,1)S(1)}, u32[]{:S(2)}, u32[]{:S(2)}) collective-permute-start(bf16[2,2,2,2,1,96,128]{6,5,3,2,1,4,0:T(8,128)(2,1)S(1)} %pad_maximum_fusion), channel_id=1, source_target_pairs={{0,1},{1,0},{2,3},{3,2},{4,5},{5,4},{6,7},{7,6},{8,9},{9,8},{10,11... | collective-permute-start | bytes 1179656 | tf_op jit(solution)/shard_map/ppermute | solution.py:26
  3.1 22.9 %collective-permute-start.1 = (bf16[2,2,2,1,2,96,128]{6,5,4,2,1,3,0:T(8,128)(2,1)S(1)}, bf16[2,2,2,1,2,96,128]{6,5,4,2,1,3,0:T(8,128)(2,1)S(1)}, u32[]{:S(2)}, u32[]{:S(2)}) collective-permute-start(bf16[2,2,2,1,2,96,128]{6,5,4,2,1,3,0:T(8,128)(2,1)S(1)} %pad_maximum_fusion.1), channel_id=1, source_target_pairs={{0,2},{2,0},{1,3},{3,1},{4,6},{6,4},{5,7},{7,5},{8,10},{10,8},{9,1... | collective-permute-start | bytes 1179656 | tf_op jit(solution)/shard_map/ppermute | solution.py:26
  5.8 13.0 %collective-permute-start.3 = (bf16[1,2,2,2,96,128]{5,4,3,2,1,0:T(8,128)(2,1)S(1)}, bf16[1,2,2,2,96,128]{5,4,3,2,1,0:T(8,128)(2,1)S(1)}, u32[]{:S(2)}, u32[]{:S(2)}) collective-permute-start(bf16[1,2,2,2,96,128]{5,4,3,2,1,0:T(8,128)(2,1)S(1)} %get-tuple-element.225), channel_id=1, source_target_pairs={{0,8},{1,9},{2,10},{3,11},{4,12},{5,13},{6,14},{7,15},{8,0},{9,1},... | collective-permute-start | bytes 589832 | tf_op jit(solution)/shard_map/ppermute | solution.py:16
  8.6 18.3 %collective-permute-start.2 = (bf16[2,2,1,2,2,96,128]{6,5,4,3,1,2,0:T(8,128)(2,1)S(1)}, bf16[2,2,1,2,2,96,128]{6,5,4,3,1,2,0:T(8,128)(2,1)S(1)}, u32[]{:S(2)}, u32[]{:S(2)}) collective-permute-start(bf16[2,2,1,2,2,96,128]{6,5,4,3,1,2,0:T(8,128)(2,1)S(1)} %pad_maximum_fusion.2), channel_id=1, source_target_pairs={{0,4},{4,0},{1,5},{5,1},{2,6},{6,2},{3,7},{7,3},{8,12},{12,8},{9,1... | collective-permute-start | bytes 1179656 | tf_op jit(solution)/shard_map/ppermute | solution.py:26
  10.3 15.4 %collective-permute-start.4 = (bf16[1,2,2,2,96,128]{5,4,3,2,1,0:T(8,128)(2,1)S(1)}, bf16[1,2,2,2,96,128]{5,4,3,2,1,0:T(8,128)(2,1)S(1)}, u32[]{:S(2)}, u32[]{:S(2)}) collective-permute-start(bf16[1,2,2,2,96,128]{5,4,3,2,1,0:T(8,128)(2,1)S(1)} %get-tuple-element.222), channel_id=1, source_target_pairs={{0,8},{1,9},{2,10},{3,11},{4,12},{5,13},{6,14},{7,15},{8,0},{9,1},... | collective-permute-start | bytes 589832 | tf_op jit(solution)/shard_map/ppermute | solution.py:16
  62.2 23.4 %copy-start.22 = (f32[16,96,128]{2,1,0:T(8,128)}, f32[16,96,128]{2,1,0:T(8,128)S(1)}, u32[]{:S(2)}) copy-start(f32[16,96,128]{2,1,0:T(8,128)S(1)} %get-tuple-element.256) | copy-start | bytes 2359300
  62.2 16.4 %collective-permute-start.5 = (bf16[2,2,2,2,1,96,128]{6,5,3,2,1,4,0:T(8,128)(2,1)S(1)}, bf16[2,2,2,2,1,96,128]{6,5,3,2,1,4,0:T(8,128)(2,1)S(1)}, u32[]{:S(2)}, u32[]{:S(2)}) collective-permute-start(bf16[2,2,2,2,1,96,128]{6,5,3,2,1,4,0:T(8,128)(2,1)S(1)} %pad_maximum_fusion.3), channel_id=1, source_target_pairs={{0,1},{1,0},{2,3},{3,2},{4,5},{5,4},{6,7},{7,6},{8,9},{9,8},{10,11... | collective-permute-start | bytes 1179656 | tf_op jit(solution)/shard_map/ppermute | solution.py:26
  62.3 12.1 %collective-permute-start.8 = (bf16[1,2,2,2,96,128]{5,4,3,2,1,0:T(8,128)(2,1)S(1)}, bf16[1,2,2,2,96,128]{5,4,3,2,1,0:T(8,128)(2,1)S(1)}, u32[]{:S(2)}, u32[]{:S(2)}) collective-permute-start(bf16[1,2,2,2,96,128]{5,4,3,2,1,0:T(8,128)(2,1)S(1)} %get-tuple-element.203), channel_id=1, source_target_pairs={{0,8},{1,9},{2,10},{3,11},{4,12},{5,13},{6,14},{7,15},{8,0},{9,1},... | collective-permute-start | bytes 589832 | tf_op jit(solution)/shard_map/ppermute | solution.py:16
  62.5 16.5 %collective-permute-start.6 = (bf16[2,2,2,1,2,96,128]{6,5,4,2,1,3,0:T(8,128)(2,1)S(1)}, bf16[2,2,2,1,2,96,128]{6,5,4,2,1,3,0:T(8,128)(2,1)S(1)}, u32[]{:S(2)}, u32[]{:S(2)}) collective-permute-start(bf16[2,2,2,1,2,96,128]{6,5,4,2,1,3,0:T(8,128)(2,1)S(1)} %pad_maximum_fusion.4), channel_id=1, source_target_pairs={{0,2},{2,0},{1,3},{3,1},{4,6},{6,4},{5,7},{7,5},{8,10},{10,8},{9,1... | collective-permute-start | bytes 1179656 | tf_op jit(solution)/shard_map/ppermute | solution.py:26
  62.5 16.1 %collective-permute-start.9 = (bf16[1,2,2,2,96,128]{5,4,3,2,1,0:T(8,128)(2,1)S(1)}, bf16[1,2,2,2,96,128]{5,4,3,2,1,0:T(8,128)(2,1)S(1)}, u32[]{:S(2)}, u32[]{:S(2)}) collective-permute-start(bf16[1,2,2,2,96,128]{5,4,3,2,1,0:T(8,128)(2,1)S(1)} %get-tuple-element.200), channel_id=1, source_target_pairs={{0,8},{1,9},{2,10},{3,11},{4,12},{5,13},{6,14},{7,15},{8,0},{9,1},... | collective-permute-start | bytes 589832 | tf_op jit(solution)/shard_map/ppermute | solution.py:16
  65.5 19.3 %collective-permute-start.7 = (bf16[2,2,1,2,2,96,128]{6,5,4,3,1,2,0:T(8,128)(2,1)S(1)}, bf16[2,2,1,2,2,96,128]{6,5,4,3,1,2,0:T(8,128)(2,1)S(1)}, u32[]{:S(2)}, u32[]{:S(2)}) collective-permute-start(bf16[2,2,1,2,2,96,128]{6,5,4,3,1,2,0:T(8,128)(2,1)S(1)} %pad_maximum_fusion.5), channel_id=1, source_target_pairs={{0,4},{4,0},{1,5},{5,1},{2,6},{6,2},{3,7},{7,3},{8,12},{12,8},{9,1... | collective-permute-start | bytes 1179656 | tf_op jit(solution)/shard_map/ppermute | solution.py:26
  87.8 62.2 %copy-start.1 = (f32[16,96,128,1]{2,1,0,3:T(8,128)}, f32[16,96,128,1]{2,1,0,3:T(8,128)S(1)}, u32[]{:S(2)}) copy-start(f32[16,96,128,1]{2,1,0,3:T(8,128)S(1)} %get-tuple-element.258) | copy-start | bytes 2359300
  151.0 23.4 %copy-start.13 = (f32[16,96,128]{2,1,0:T(8,128)}, f32[16,96,128]{2,1,0:T(8,128)S(1)}, u32[]{:S(2)}) copy-start(f32[16,96,128]{2,1,0:T(8,128)S(1)} %get-tuple-element.62) | copy-start | bytes 2359300
  151.0 16.4 %collective-permute-start.10 = (bf16[2,2,2,2,1,96,128]{6,5,3,2,1,4,0:T(8,128)(2,1)S(1)}, bf16[2,2,2,2,1,96,128]{6,5,3,2,1,4,0:T(8,128)(2,1)S(1)}, u32[]{:S(2)}, u32[]{:S(2)}) collective-permute-start(bf16[2,2,2,2,1,96,128]{6,5,3,2,1,4,0:T(8,128)(2,1)S(1)} %pad_maximum_fusion.6), channel_id=1, source_target_pairs={{0,1},{1,0},{2,3},{3,2},{4,5},{5,4},{6,7},{7,6},{8,9},{9,8},{10,11... | collective-permute-start | bytes 1179656 | tf_op jit(solution)/shard_map/ppermute | solution.py:26
  151.1 12.1 %collective-permute-start.13 = (bf16[1,2,2,2,96,128]{5,4,3,2,1,0:T(8,128)(2,1)S(1)}, bf16[1,2,2,2,96,128]{5,4,3,2,1,0:T(8,128)(2,1)S(1)}, u32[]{:S(2)}, u32[]{:S(2)}) collective-permute-start(bf16[1,2,2,2,96,128]{5,4,3,2,1,0:T(8,128)(2,1)S(1)} %get-tuple-element.181), channel_id=1, source_target_pairs={{0,8},{1,9},{2,10},{3,11},{4,12},{5,13},{6,14},{7,15},{8,0},{9,1},... | collective-permute-start | bytes 589832 | tf_op jit(solution)/shard_map/ppermute | solution.py:16
  151.2 16.5 %collective-permute-start.11 = (bf16[2,2,2,1,2,96,128]{6,5,4,2,1,3,0:T(8,128)(2,1)S(1)}, bf16[2,2,2,1,2,96,128]{6,5,4,2,1,3,0:T(8,128)(2,1)S(1)}, u32[]{:S(2)}, u32[]{:S(2)}) collective-permute-start(bf16[2,2,2,1,2,96,128]{6,5,4,2,1,3,0:T(8,128)(2,1)S(1)} %pad_maximum_fusion.7), channel_id=1, source_target_pairs={{0,2},{2,0},{1,3},{3,1},{4,6},{6,4},{5,7},{7,5},{8,10},{10,8},{9,1... | collective-permute-start | bytes 1179656 | tf_op jit(solution)/shard_map/ppermute | solution.py:26
  151.3 16.1 %collective-permute-start.14 = (bf16[1,2,2,2,96,128]{5,4,3,2,1,0:T(8,128)(2,1)S(1)}, bf16[1,2,2,2,96,128]{5,4,3,2,1,0:T(8,128)(2,1)S(1)}, u32[]{:S(2)}, u32[]{:S(2)}) collective-permute-start(bf16[1,2,2,2,96,128]{5,4,3,2,1,0:T(8,128)(2,1)S(1)} %get-tuple-element.178), channel_id=1, source_target_pairs={{0,8},{1,9},{2,10},{3,11},{4,12},{5,13},{6,14},{7,15},{8,0},{9,1},... | collective-permute-start | bytes 589832 | tf_op jit(solution)/shard_map/ppermute | solution.py:16
  154.3 19.3 %collective-permute-start.12 = (bf16[2,2,1,2,2,96,128]{6,5,4,3,1,2,0:T(8,128)(2,1)S(1)}, bf16[2,2,1,2,2,96,128]{6,5,4,3,1,2,0:T(8,128)(2,1)S(1)}, u32[]{:S(2)}, u32[]{:S(2)}) collective-permute-start(bf16[2,2,1,2,2,96,128]{6,5,4,3,1,2,0:T(8,128)(2,1)S(1)} %pad_maximum_fusion.8), channel_id=1, source_target_pairs={{0,4},{4,0},{1,5},{5,1},{2,6},{6,2},{3,7},{7,3},{8,12},{12,8},{9,1... | collective-permute-start | bytes 1179656 | tf_op jit(solution)/shard_map/ppermute | solution.py:26
  241.4 23.4 %copy-start.17 = (f32[16,96,128]{2,1,0:T(8,128)}, f32[16,96,128]{2,1,0:T(8,128)S(1)}, u32[]{:S(2)}) copy-start(f32[16,96,128]{2,1,0:T(8,128)S(1)} %get-tuple-element.59) | copy-start | bytes 2359300
  241.4 16.4 %collective-permute-start.15 = (bf16[2,2,2,2,1,96,128]{6,5,3,2,1,4,0:T(8,128)(2,1)S(1)}, bf16[2,2,2,2,1,96,128]{6,5,3,2,1,4,0:T(8,128)(2,1)S(1)}, u32[]{:S(2)}, u32[]{:S(2)}) collective-permute-start(bf16[2,2,2,2,1,96,128]{6,5,3,2,1,4,0:T(8,128)(2,1)S(1)} %pad_maximum_fusion.9), channel_id=1, source_target_pairs={{0,1},{1,0},{2,3},{3,2},{4,5},{5,4},{6,7},{7,6},{8,9},{9,8},{10,11... | collective-permute-start | bytes 1179656 | tf_op jit(solution)/shard_map/ppermute | solution.py:26
  241.5 12.1 %collective-permute-start.18 = (bf16[1,2,2,2,96,128]{5,4,3,2,1,0:T(8,128)(2,1)S(1)}, bf16[1,2,2,2,96,128]{5,4,3,2,1,0:T(8,128)(2,1)S(1)}, u32[]{:S(2)}, u32[]{:S(2)}) collective-permute-start(bf16[1,2,2,2,96,128]{5,4,3,2,1,0:T(8,128)(2,1)S(1)} %get-tuple-element.159), channel_id=1, source_target_pairs={{0,8},{1,9},{2,10},{3,11},{4,12},{5,13},{6,14},{7,15},{8,0},{9,1},... | collective-permute-start | bytes 589832 | tf_op jit(solution)/shard_map/ppermute | solution.py:16
  241.6 16.5 %collective-permute-start.16 = (bf16[2,2,2,1,2,96,128]{6,5,4,2,1,3,0:T(8,128)(2,1)S(1)}, bf16[2,2,2,1,2,96,128]{6,5,4,2,1,3,0:T(8,128)(2,1)S(1)}, u32[]{:S(2)}, u32[]{:S(2)}) collective-permute-start(bf16[2,2,2,1,2,96,128]{6,5,4,2,1,3,0:T(8,128)(2,1)S(1)} %pad_maximum_fusion.10), channel_id=1, source_target_pairs={{0,2},{2,0},{1,3},{3,1},{4,6},{6,4},{5,7},{7,5},{8,10},{10,8},{9,1... | collective-permute-start | bytes 1179656 | tf_op jit(solution)/shard_map/ppermute | solution.py:26
  241.7 16.1 %collective-permute-start.19 = (bf16[1,2,2,2,96,128]{5,4,3,2,1,0:T(8,128)(2,1)S(1)}, bf16[1,2,2,2,96,128]{5,4,3,2,1,0:T(8,128)(2,1)S(1)}, u32[]{:S(2)}, u32[]{:S(2)}) collective-permute-start(bf16[1,2,2,2,96,128]{5,4,3,2,1,0:T(8,128)(2,1)S(1)} %get-tuple-element.156), channel_id=1, source_target_pairs={{0,8},{1,9},{2,10},{3,11},{4,12},{5,13},{6,14},{7,15},{8,0},{9,1},... | collective-permute-start | bytes 589832 | tf_op jit(solution)/shard_map/ppermute | solution.py:16
  244.7 19.3 %collective-permute-start.17 = (bf16[2,2,1,2,2,96,128]{6,5,4,3,1,2,0:T(8,128)(2,1)S(1)}, bf16[2,2,1,2,2,96,128]{6,5,4,3,1,2,0:T(8,128)(2,1)S(1)}, u32[]{:S(2)}, u32[]{:S(2)}) collective-permute-start(bf16[2,2,1,2,2,96,128]{6,5,4,3,1,2,0:T(8,128)(2,1)S(1)} %pad_maximum_fusion.11), channel_id=1, source_target_pairs={{0,4},{4,0},{1,5},{5,1},{2,6},{6,2},{3,7},{7,3},{8,12},{12,8},{9,1... | collective-permute-start | bytes 1179656 | tf_op jit(solution)/shard_map/ppermute | solution.py:26
  336.1 23.4 %copy-start.26 = (f32[16,96,128]{2,1,0:T(8,128)}, f32[16,96,128]{2,1,0:T(8,128)S(1)}, u32[]{:S(2)}) copy-start(f32[16,96,128]{2,1,0:T(8,128)S(1)} %get-tuple-element.55) | copy-start | bytes 2359300
  336.2 16.4 %collective-permute-start.20 = (bf16[2,2,2,2,1,96,128]{6,5,3,2,1,4,0:T(8,128)(2,1)S(1)}, bf16[2,2,2,2,1,96,128]{6,5,3,2,1,4,0:T(8,128)(2,1)S(1)}, u32[]{:S(2)}, u32[]{:S(2)}) collective-permute-start(bf16[2,2,2,2,1,96,128]{6,5,3,2,1,4,0:T(8,128)(2,1)S(1)} %pad_maximum_fusion.12), channel_id=1, source_target_pairs={{0,1},{1,0},{2,3},{3,2},{4,5},{5,4},{6,7},{7,6},{8,9},{9,8},{10,11... | collective-permute-start | bytes 1179656 | tf_op jit(solution)/shard_map/ppermute | solution.py:26
  336.2 12.1 %collective-permute-start.23 = (bf16[1,2,2,2,96,128]{5,4,3,2,1,0:T(8,128)(2,1)S(1)}, bf16[1,2,2,2,96,128]{5,4,3,2,1,0:T(8,128)(2,1)S(1)}, u32[]{:S(2)}, u32[]{:S(2)}) collective-permute-start(bf16[1,2,2,2,96,128]{5,4,3,2,1,0:T(8,128)(2,1)S(1)} %get-tuple-element.137), channel_id=1, source_target_pairs={{0,8},{1,9},{2,10},{3,11},{4,12},{5,13},{6,14},{7,15},{8,0},{9,1},... | collective-permute-start | bytes 589832 | tf_op jit(solution)/shard_map/ppermute | solution.py:16
  336.4 16.5 %collective-permute-start.21 = (bf16[2,2,2,1,2,96,128]{6,5,4,2,1,3,0:T(8,128)(2,1)S(1)}, bf16[2,2,2,1,2,96,128]{6,5,4,2,1,3,0:T(8,128)(2,1)S(1)}, u32[]{:S(2)}, u32[]{:S(2)}) collective-permute-start(bf16[2,2,2,1,2,96,128]{6,5,4,2,1,3,0:T(8,128)(2,1)S(1)} %pad_maximum_fusion.13), channel_id=1, source_target_pairs={{0,2},{2,0},{1,3},{3,1},{4,6},{6,4},{5,7},{7,5},{8,10},{10,8},{9,1... | collective-permute-start | bytes 1179656 | tf_op jit(solution)/shard_map/ppermute | solution.py:26
  336.4 16.1 %collective-permute-start.24 = (bf16[1,2,2,2,96,128]{5,4,3,2,1,0:T(8,128)(2,1)S(1)}, bf16[1,2,2,2,96,128]{5,4,3,2,1,0:T(8,128)(2,1)S(1)}, u32[]{:S(2)}, u32[]{:S(2)}) collective-permute-start(bf16[1,2,2,2,96,128]{5,4,3,2,1,0:T(8,128)(2,1)S(1)} %get-tuple-element.134), channel_id=1, source_target_pairs={{0,8},{1,9},{2,10},{3,11},{4,12},{5,13},{6,14},{7,15},{8,0},{9,1},... | collective-permute-start | bytes 589832 | tf_op jit(solution)/shard_map/ppermute | solution.py:16
  339.4 19.3 %collective-permute-start.22 = (bf16[2,2,1,2,2,96,128]{6,5,4,3,1,2,0:T(8,128)(2,1)S(1)}, bf16[2,2,1,2,2,96,128]{6,5,4,3,1,2,0:T(8,128)(2,1)S(1)}, u32[]{:S(2)}, u32[]{:S(2)}) collective-permute-start(bf16[2,2,1,2,2,96,128]{6,5,4,3,1,2,0:T(8,128)(2,1)S(1)} %pad_maximum_fusion.14), channel_id=1, source_target_pairs={{0,4},{4,0},{1,5},{5,1},{2,6},{6,2},{3,7},{7,3},{8,12},{12,8},{9,1... | collective-permute-start | bytes 1179656 | tf_op jit(solution)/shard_map/ppermute | solution.py:26
  362.6 239.2 %copy-start.5 = (f32[16,96,128]{2,1,0:T(8,128)}, f32[16,96,128]{2,1,0:T(8,128)S(1)}, u32[]{:S(2)}) copy-start(f32[16,96,128]{2,1,0:T(8,128)S(1)} %get-tuple-element.51) | copy-start | bytes 2359300
  394.7 16.4 %collective-permute-start.25 = (bf16[2,2,2,2,1,96,128]{6,5,3,2,1,4,0:T(8,128)(2,1)S(1)}, bf16[2,2,2,2,1,96,128]{6,5,3,2,1,4,0:T(8,128)(2,1)S(1)}, u32[]{:S(2)}, u32[]{:S(2)}) collective-permute-start(bf16[2,2,2,2,1,96,128]{6,5,3,2,1,4,0:T(8,128)(2,1)S(1)} %pad_maximum_fusion.15), channel_id=1, source_target_pairs={{0,1},{1,0},{2,3},{3,2},{4,5},{5,4},{6,7},{7,6},{8,9},{9,8},{10,11... | collective-permute-start | bytes 1179656 | tf_op jit(solution)/shard_map/ppermute | solution.py:26
  394.8 12.1 %collective-permute-start.28 = (bf16[1,2,2,2,96,128]{5,4,3,2,1,0:T(8,128)(2,1)S(1)}, bf16[1,2,2,2,96,128]{5,4,3,2,1,0:T(8,128)(2,1)S(1)}, u32[]{:S(2)}, u32[]{:S(2)}) collective-permute-start(bf16[1,2,2,2,96,128]{5,4,3,2,1,0:T(8,128)(2,1)S(1)} %get-tuple-element.115), channel_id=1, source_target_pairs={{0,8},{1,9},{2,10},{3,11},{4,12},{5,13},{6,14},{7,15},{8,0},{9,1},... | collective-permute-start | bytes 589832 | tf_op jit(solution)/shard_map/ppermute | solution.py:16
  394.9 16.5 %collective-permute-start.26 = (bf16[2,2,2,1,2,96,128]{6,5,4,2,1,3,0:T(8,128)(2,1)S(1)}, bf16[2,2,2,1,2,96,128]{6,5,4,2,1,3,0:T(8,128)(2,1)S(1)}, u32[]{:S(2)}, u32[]{:S(2)}) collective-permute-start(bf16[2,2,2,1,2,96,128]{6,5,4,2,1,3,0:T(8,128)(2,1)S(1)} %pad_maximum_fusion.16), channel_id=1, source_target_pairs={{0,2},{2,0},{1,3},{3,1},{4,6},{6,4},{5,7},{7,5},{8,10},{10,8},{9,1... | collective-permute-start | bytes 1179656 | tf_op jit(solution)/shard_map/ppermute | solution.py:26
  395.0 16.1 %collective-permute-start.29 = (bf16[1,2,2,2,96,128]{5,4,3,2,1,0:T(8,128)(2,1)S(1)}, bf16[1,2,2,2,96,128]{5,4,3,2,1,0:T(8,128)(2,1)S(1)}, u32[]{:S(2)}, u32[]{:S(2)}) collective-permute-start(bf16[1,2,2,2,96,128]{5,4,3,2,1,0:T(8,128)(2,1)S(1)} %get-tuple-element.112), channel_id=1, source_target_pairs={{0,8},{1,9},{2,10},{3,11},{4,12},{5,13},{6,14},{7,15},{8,0},{9,1},... | collective-permute-start | bytes 589832 | tf_op jit(solution)/shard_map/ppermute | solution.py:16
  398.0 19.3 %collective-permute-start.27 = (bf16[2,2,1,2,2,96,128]{6,5,4,3,1,2,0:T(8,128)(2,1)S(1)}, bf16[2,2,1,2,2,96,128]{6,5,4,3,1,2,0:T(8,128)(2,1)S(1)}, u32[]{:S(2)}, u32[]{:S(2)}) collective-permute-start(bf16[2,2,1,2,2,96,128]{6,5,4,3,1,2,0:T(8,128)(2,1)S(1)} %pad_maximum_fusion.17), channel_id=1, source_target_pairs={{0,4},{4,0},{1,5},{5,1},{2,6},{6,2},{3,7},{7,3},{8,12},{12,8},{9,1... | collective-permute-start | bytes 1179656 | tf_op jit(solution)/shard_map/ppermute | solution.py:26
  486.3 16.4 %collective-permute-start.30 = (bf16[2,2,2,2,1,96,128]{6,5,3,2,1,4,0:T(8,128)(2,1)S(1)}, bf16[2,2,2,2,1,96,128]{6,5,3,2,1,4,0:T(8,128)(2,1)S(1)}, u32[]{:S(2)}, u32[]{:S(2)}) collective-permute-start(bf16[2,2,2,2,1,96,128]{6,5,3,2,1,4,0:T(8,128)(2,1)S(1)} %pad_maximum_fusion.18), channel_id=1, source_target_pairs={{0,1},{1,0},{2,3},{3,2},{4,5},{5,4},{6,7},{7,6},{8,9},{9,8},{10,11... | collective-permute-start | bytes 1179656 | tf_op jit(solution)/shard_map/ppermute | solution.py:26
  486.3 12.1 %collective-permute-start.33 = (bf16[1,2,2,2,96,128]{5,4,3,2,1,0:T(8,128)(2,1)S(1)}, bf16[1,2,2,2,96,128]{5,4,3,2,1,0:T(8,128)(2,1)S(1)}, u32[]{:S(2)}, u32[]{:S(2)}) collective-permute-start(bf16[1,2,2,2,96,128]{5,4,3,2,1,0:T(8,128)(2,1)S(1)} %get-tuple-element.93), channel_id=1, source_target_pairs={{0,8},{1,9},{2,10},{3,11},{4,12},{5,13},{6,14},{7,15},{8,0},{9,1},... | collective-permute-start | bytes 589832 | tf_op jit(solution)/shard_map/ppermute | solution.py:16
  486.5 16.5 %collective-permute-start.31 = (bf16[2,2,2,1,2,96,128]{6,5,4,2,1,3,0:T(8,128)(2,1)S(1)}, bf16[2,2,2,1,2,96,128]{6,5,4,2,1,3,0:T(8,128)(2,1)S(1)}, u32[]{:S(2)}, u32[]{:S(2)}) collective-permute-start(bf16[2,2,2,1,2,96,128]{6,5,4,2,1,3,0:T(8,128)(2,1)S(1)} %pad_maximum_fusion.19), channel_id=1, source_target_pairs={{0,2},{2,0},{1,3},{3,1},{4,6},{6,4},{5,7},{7,5},{8,10},{10,8},{9,1... | collective-permute-start | bytes 1179656 | tf_op jit(solution)/shard_map/ppermute | solution.py:26
  486.6 16.1 %collective-permute-start.34 = (bf16[1,2,2,2,96,128]{5,4,3,2,1,0:T(8,128)(2,1)S(1)}, bf16[1,2,2,2,96,128]{5,4,3,2,1,0:T(8,128)(2,1)S(1)}, u32[]{:S(2)}, u32[]{:S(2)}) collective-permute-start(bf16[1,2,2,2,96,128]{5,4,3,2,1,0:T(8,128)(2,1)S(1)} %get-tuple-element.90), channel_id=1, source_target_pairs={{0,8},{1,9},{2,10},{3,11},{4,12},{5,13},{6,14},{7,15},{8,0},{9,1},... | collective-permute-start | bytes 589832 | tf_op jit(solution)/shard_map/ppermute | solution.py:16
  489.6 19.3 %collective-permute-start.32 = (bf16[2,2,1,2,2,96,128]{6,5,4,3,1,2,0:T(8,128)(2,1)S(1)}, bf16[2,2,1,2,2,96,128]{6,5,4,3,1,2,0:T(8,128)(2,1)S(1)}, u32[]{:S(2)}, u32[]{:S(2)}) collective-permute-start(bf16[2,2,1,2,2,96,128]{6,5,4,3,1,2,0:T(8,128)(2,1)S(1)} %pad_maximum_fusion.20), channel_id=1, source_target_pairs={{0,4},{4,0},{1,5},{5,1},{2,6},{6,2},{3,7},{7,3},{8,12},{12,8},{9,1... | collective-permute-start | bytes 1179656 | tf_op jit(solution)/shard_map/ppermute | solution.py:26
  578.5 23.4 %copy-start.24 = (f32[16,96,128]{2,1,0:T(8,128)}, f32[16,96,128]{2,1,0:T(8,128)S(1)}, u32[]{:S(2)}) copy-start(f32[16,96,128]{2,1,0:T(8,128)S(1)} %get-tuple-element.44) | copy-start | bytes 2359300
  578.5 16.4 %collective-permute-start.35 = (bf16[2,2,2,2,1,96,128]{6,5,3,2,1,4,0:T(8,128)(2,1)S(1)}, bf16[2,2,2,2,1,96,128]{6,5,3,2,1,4,0:T(8,128)(2,1)S(1)}, u32[]{:S(2)}, u32[]{:S(2)}) collective-permute-start(bf16[2,2,2,2,1,96,128]{6,5,3,2,1,4,0:T(8,128)(2,1)S(1)} %pad_maximum_fusion.21), channel_id=1, source_target_pairs={{0,1},{1,0},{2,3},{3,2},{4,5},{5,4},{6,7},{7,6},{8,9},{9,8},{10,11... | collective-permute-start | bytes 1179656 | tf_op jit(solution)/shard_map/ppermute | solution.py:26
  578.6 12.1 %collective-permute-start.38 = (bf16[1,2,2,2,96,128]{5,4,3,2,1,0:T(8,128)(2,1)S(1)}, bf16[1,2,2,2,96,128]{5,4,3,2,1,0:T(8,128)(2,1)S(1)}, u32[]{:S(2)}, u32[]{:S(2)}) collective-permute-start(bf16[1,2,2,2,96,128]{5,4,3,2,1,0:T(8,128)(2,1)S(1)} %get-tuple-element.71), channel_id=1, source_target_pairs={{0,8},{1,9},{2,10},{3,11},{4,12},{5,13},{6,14},{7,15},{8,0},{9,1},... | collective-permute-start | bytes 589832 | tf_op jit(solution)/shard_map/ppermute | solution.py:16
  578.7 16.5 %collective-permute-start.36 = (bf16[2,2,2,1,2,96,128]{6,5,4,2,1,3,0:T(8,128)(2,1)S(1)}, bf16[2,2,2,1,2,96,128]{6,5,4,2,1,3,0:T(8,128)(2,1)S(1)}, u32[]{:S(2)}, u32[]{:S(2)}) collective-permute-start(bf16[2,2,2,1,2,96,128]{6,5,4,2,1,3,0:T(8,128)(2,1)S(1)} %pad_maximum_fusion.22), channel_id=1, source_target_pairs={{0,2},{2,0},{1,3},{3,1},{4,6},{6,4},{5,7},{7,5},{8,10},{10,8},{9,1... | collective-permute-start | bytes 1179656 | tf_op jit(solution)/shard_map/ppermute | solution.py:26
  578.8 16.1 %collective-permute-start.39 = (bf16[1,2,2,2,96,128]{5,4,3,2,1,0:T(8,128)(2,1)S(1)}, bf16[1,2,2,2,96,128]{5,4,3,2,1,0:T(8,128)(2,1)S(1)}, u32[]{:S(2)}, u32[]{:S(2)}) collective-permute-start(bf16[1,2,2,2,96,128]{5,4,3,2,1,0:T(8,128)(2,1)S(1)} %get-tuple-element.68), channel_id=1, source_target_pairs={{0,8},{1,9},{2,10},{3,11},{4,12},{5,13},{6,14},{7,15},{8,0},{9,1},... | collective-permute-start | bytes 589832 | tf_op jit(solution)/shard_map/ppermute | solution.py:16
  581.8 19.3 %collective-permute-start.37 = (bf16[2,2,1,2,2,96,128]{6,5,4,3,1,2,0:T(8,128)(2,1)S(1)}, bf16[2,2,1,2,2,96,128]{6,5,4,3,1,2,0:T(8,128)(2,1)S(1)}, u32[]{:S(2)}, u32[]{:S(2)}) collective-permute-start(bf16[2,2,1,2,2,96,128]{6,5,4,3,1,2,0:T(8,128)(2,1)S(1)} %pad_maximum_fusion.23), channel_id=1, source_target_pairs={{0,4},{4,0},{1,5},{5,1},{2,6},{6,2},{3,7},{7,3},{8,12},{12,8},{9,1... | collective-permute-start | bytes 1179656 | tf_op jit(solution)/shard_map/ppermute | solution.py:26
  605.6 62.2 %copy-start.2 = (f32[16,96,128,1]{2,1,0,3:T(8,128)S(1)}, f32[16,96,128,1]{2,1,0,3:T(8,128)}, u32[]{:S(2)}) copy-start(f32[16,96,128,1]{2,1,0,3:T(8,128)} %copy-done.1) | copy-start | bytes 2359300
  (37 other events, 159.1 us)
where the time goes:
time: 683 us; the launch traced here: 676 us
  blocking collectives  415 us (61%)
  waiting for transfers between devices  145 us (21%)
  other arithmetic  46.6 us (7%)
  starting transfers between devices  30.5 us (4%)
  matrix products  19.7 us (3%)
  local copies, waits for them, and re-layouts  15.5 us (2%)
    psum x8, blocking collectives, solve(): lax.psum((dot_fields(image, image), dot_fields(image, residual)), 'ta')  238 us
    psum x6, blocking collectives, solve(): heights = lax.psum(local_heights, 'ta')  177 us
    ppermute x16, waiting for transfers between devices, passed_along(): return lax.ppermute(value, axis, pairs)  105 us
    ppermute x24, waiting for transfers between devices, from_partner(): return lax.ppermute(block, axis, route)  39.9 us
    ppermute x16, starting transfers between devices, passed_along(): return lax.ppermute(value, axis, pairs)  24.3 us
    dot_general x8, matrix products, operate(): jnp.einsum('skri,skoi->sro', flat_stack, flat_blocks, preferred_element_t...  19.7 us
    reduce_sum x7, other arithmetic, dot_fields(): return jnp.sum(first * second, axis=(0, 1, 2, 3, 5))  17 us
    convert_element_type x8, other arithmetic, operate(): rounded = field.astype(jnp.bfloat16)  14.5 us
  transfers between devices with their start and end apart: 40, of which 24 were waited for; matrix products, arithmetic and copies ran while one was open for 1% of the time, Pallas kernels for 0%

commit v1 on v0

v1 whole, which is shorter than its diff:
```python
import functools

import jax
import jax.numpy as jnp
from jax import lax
from jax.experimental import pallas as pl
from jax.experimental.pallas import tpu as pltpu
from jax.sharding import PartitionSpec as P

CYCLES = 2
KRYLOV = 4
PARTS = 2
UNROLL = 1

mass_term = 3.5
MESH = pl.DeviceIdType.MESH


def dot_t(left, right):
    return lax.dot_general(
        left, right, (((1,), (1,)), ((), ())), preferred_element_type=jnp.float32
    )


def kernel(
    n, src, blocks, sol, res, w, halo, dirs, imgs, sbuf, rbuf,
    halo_send, halo_recv, red_send, red_recv,
):
    sites, rhs, width = src.shape
    rows = rhs // PARTS
    half = sites // 2
    me = lax.axis_index("ta")
    group = lax.axis_index("groups")

    barrier = pltpu.get_barrier_semaphore()

    def peers(body):
        if n <= 16:
            for j in range(1, n):
                body(j)
        else:
            lax.fori_loop(1, n, lambda j, c: (body(j), c)[1], 0)

    def peer_at(j):
        return (group, lax.rem(me + j, n))

    peers(lambda j: pl.semaphore_signal(
        barrier, inc=1, device_id=peer_at(j), device_id_type=MESH))

    def flip(bit):
        step = 1 << bit
        return me + step - 2 * step * (lax.rem(me // step, 2))

    def halo_copies(p):
        ahead = lax.rem(me + 8, n)
        behind = lax.rem(me + n - 8, n)

        def one(src_ref, dst_ref, index, device):
            return pltpu.make_async_remote_copy(
                src_ref=src_ref, dst_ref=dst_ref,
                send_sem=halo_send.at[p, index], recv_sem=halo_recv.at[p, index],
                device_id=(group, device), device_id_type=MESH)

        copies = [
            one(w.at[p, pl.ds(half, half)], halo.at[3, p, pl.ds(half, half)], 3, ahead),
            one(w.at[p, pl.ds(0, half)], halo.at[3, p, pl.ds(0, half)], 4, behind),
        ]
        for bit in (2, 1, 0):
            copies.append(one(w.at[p], halo.at[bit, p], bit, flip(bit)))
        return copies

    def start_halo(p):
        for copy in halo_copies(p):
            copy.start()

    def rs(p):
        return pl.ds(p * rows, rows)

    eye = (lax.broadcasted_iota(jnp.int32, (rows, 128), 0)
           == lax.broadcasted_iota(jnp.int32, (rows, 128), 1))
    sub = lax.broadcasted_iota(jnp.int32, (8, 128), 0)

    def to_row(partial):
        column = jnp.sum(partial, axis=1, keepdims=True)
        return jnp.sum(jnp.where(eye, column, 0.0), axis=0, keepdims=True)

    def to_column(row):
        return jnp.sum(jnp.where(eye, row, 0.0), axis=1, keepdims=True)

    counter = [0]

    def reduce_start(partials):
        q = counter[0] % 2
        counter[0] += 1
        tile = jnp.zeros((8, 128), jnp.float32)
        for i, partial in enumerate(partials):
            tile = jnp.where(sub == i, to_row(partial), tile)
        sbuf[q] = tile

        def send(j):
            pltpu.make_async_remote_copy(
                src_ref=sbuf.at[q], dst_ref=rbuf.at[q, j - 1],
                send_sem=red_send.at[q], recv_sem=red_recv.at[q],
                device_id=peer_at(j), device_id_type=MESH).start()

        peers(send)
        return q, tile

    def reduce_end(handle):
        q, tile = handle
        pltpu.make_async_remote_copy(
            src_ref=rbuf.at[q], dst_ref=rbuf.at[q],
            send_sem=red_send.at[q], recv_sem=red_recv.at[q],
            device_id=peer_at(1), device_id_type=MESH).wait()
        return tile + jnp.sum(rbuf[q], axis=0)

    def over_sites(body, carry):
        def step(i, c):
            for q in range(UNROLL):
                c = body(i * UNROLL + q, i, q, c)
            return c
        return lax.fori_loop(0, sites // UNROLL, step, carry)

    def bit_of(i, q, bit):
        if (1 << bit) < UNROLL:
            return (q >> bit) & 1
        return lax.rem(i // ((1 << bit) // UNROLL), 2)

    def hop_terms(s, i, q, field_of, other):
        lefts, rights = [], []
        for bit in range(4):
            b = bit_of(i, q, bit)
            mate = s + (1 << bit) - 2 * (1 << bit) * b
            k = 2 + 2 * bit - b if other else 1 + 2 * bit + b
            lefts.append(field_of(bit, mate))
            rights.append(blocks[s, k])
        return dot_t(jnp.concatenate(lefts, axis=1), jnp.concatenate(rights, axis=1))

    def local_part(p, slot):
        def body(s, i, q, c):
            hops = hop_terms(s, i, q, lambda bit, m: w[p, m], False)
            own = dot_t(w[p, s], blocks[s, 0])
            imgs[slot, s, rs(p)] = mass_term * res[s, rs(p)] + own - hops
            return c
        over_sites(body, 0)

    zero = jnp.zeros((rows, width), jnp.float32)

    def process(p, k, norms, last):
        for copy in halo_copies(p):
            copy.wait_recv()

        def apply(s, i, q, c):
            hops = hop_terms(s, i, q, lambda bit, m: halo[bit, p, m], True)
            image = imgs[k, s, rs(p)] - hops
            imgs[k, s, rs(p)] = image
            if k == 0:
                return (c[0] + image * image, c[1] + image * res[s, rs(p)])
            return tuple(c[j] + image * imgs[j, s, rs(p)] for j in range(k))

        sums = over_sites(apply, (zero,) * (k if k else 2))
        if k:
            total = reduce_end(reduce_start(sums))
            factors = [to_column(total[j:j + 1] / norms[j]) for j in range(k)]

            def orthogonal(s, i, q, c):
                image = imgs[k, s, rs(p)]
                for j in range(k):
                    image = image - factors[j] * imgs[j, s, rs(p)]
                imgs[k, s, rs(p)] = image
                return (c[0] + image * image, c[1] + image * res[s, rs(p)])

            sums = over_sites(orthogonal, (zero, zero))
        handle = reduce_start(sums)

        def steer(s, i, q, c):
            direction = res[s, rs(p)]
            for j in range(k):
                direction = direction - factors[j] * dirs[j, s, rs(p)]
            dirs[k, s, rs(p)] = direction
            return c

        over_sites(steer, 0)
        for copy in halo_copies(p):
            copy.wait_send()
        total = reduce_end(handle)
        norm = total[0:1]
        alpha = to_column(total[1:2] / norm)

        def shrink(s, i, q, c):
            residual = res[s, rs(p)] - alpha * imgs[k, s, rs(p)]
            res[s, rs(p)] = residual
            w[p, s] = residual.astype(jnp.bfloat16)
            return c

        over_sites(shrink, 0)

        def advance(s, i, q, c):
            sol[s, rs(p)] = sol[s, rs(p)] + alpha * dirs[k, s, rs(p)]
            return c

        def go_on():
            start_halo(p)

        def prepare():
            local_part(p, (k + 1) % KRYLOV)

        if last is None:
            go_on()
            over_sites(advance, 0)
            prepare()
        else:
            pl.when(jnp.logical_not(last))(go_on)
            over_sites(advance, 0)
            pl.when(jnp.logical_not(last))(prepare)
        return norms + [norm]

    def fill(s, i, q, c):
        value = src[s]
        res[s] = value
        sol[s] = jnp.zeros_like(value)
        for p in range(PARTS):
            w[p, s] = value[p * rows:(p + 1) * rows].astype(jnp.bfloat16)
        return c

    over_sites(fill, 0)
    pl.semaphore_wait(barrier, n - 1)
    for p in range(PARTS):
        start_halo(p)
    for p in range(PARTS):
        local_part(p, 0)

    def cycle(index, c):
        norms = [[] for _ in range(PARTS)]
        for k in range(KRYLOV):
            for p in range(PARTS):
                last = index == CYCLES - 1 if k == KRYLOV - 1 else None
                norms[p] = process(p, k, norms[p], last)
        return c

    lax.fori_loop(0, CYCLES, cycle, 0)


def shards(sources, coarse_blocks):
    n = lax.axis_size("ta")
    shape = sources.shape
    rhs, width = shape[5], shape[6]
    sites = shape[1] * shape[2] * shape[3] * shape[4]
    count = coarse_blocks.shape[5]
    rows = rhs // PARTS
    field = jax.ShapeDtypeStruct((sites, rhs, width), jnp.float32)
    vmem = pl.BlockSpec(memory_space=pltpu.VMEM)
    solution, residual = pl.pallas_call(
        functools.partial(kernel, n),
        out_shape=(field, field),
        in_specs=[vmem, vmem],
        out_specs=(vmem, vmem),
        scratch_shapes=[
            pltpu.VMEM((PARTS, sites, rows, width), jnp.bfloat16),
            pltpu.VMEM((4, PARTS, sites, rows, width), jnp.bfloat16),
            pltpu.VMEM((KRYLOV, sites, rhs, width), jnp.float32),
            pltpu.VMEM((KRYLOV, sites, rhs, width), jnp.float32),
            pltpu.VMEM((2, 8, 128), jnp.float32),
            pltpu.VMEM((2, n - 1, 8, 128), jnp.float32),
            pltpu.SemaphoreType.DMA((PARTS, 5)),
            pltpu.SemaphoreType.DMA((PARTS, 5)),
            pltpu.SemaphoreType.DMA((2,)),
            pltpu.SemaphoreType.DMA((2,)),
        ],
        compiler_params=pltpu.CompilerParams(
            collective_id=0, has_side_effects=True, vmem_limit_bytes=40 << 20
        ),
    )(
        sources.reshape(sites, rhs, width),
        coarse_blocks.reshape(sites, count, width, width),
    )
    return solution.reshape(shape), residual.reshape(shape)


def solution(mesh):
    placed = (
        P(("groups", "ta"), None, None, None, None, None, None),
        P(("groups", "ta"), None, None, None, None, None, None, None),
    )
    return jax.shard_map(
        shards,
        mesh=mesh,
        in_specs=placed,
        out_specs=(
            P(("groups", "ta"), None, None, None, None, None, None),
            P(("groups", "ta"), None, None, None, None, None, None),
        ),
        check_vma=False,
    )
```

time: 683 us -> 276 us (0.40)
  blocking collectives: 415 us -> 0 us
  Pallas kernels: 0 us -> 270 us
  waiting for transfers between devices: 145 us -> 0 us
  other arithmetic: 46.6 us -> 0 us
  starting transfers between devices: 30.5 us -> 0 us
  matrix products: 19.7 us -> 0 us
  local copies, waits for them, and re-layouts: 15.5 us -> 5.22 us
    psum x14 -> x0, blocking collectives: 415 us -> none  [the longest x8 238 us: solve(): lax.psum((dot_fields(image, image), dot_fields(image, residual)), 'ta')]
    pallas_call x0 -> x1, Pallas kernels: none -> 270 us  [shards(): pl.pallas_call(functools.partial(kernel, n), out_shape=(field, field), in...]
    ppermute x40 -> x0, waiting for transfers between devices: 145 us -> none  [the longest x16 105 us: passed_along(): return lax.ppermute(value, axis, pairs)]
    ppermute x40 -> x0, starting transfers between devices: 30.5 us -> none  [the longest x16 24.3 us: passed_along(): return lax.ppermute(value, axis, pairs)]
    dot_general x8 -> x0, matrix products: 19.7 us -> none  [operate(): jnp.einsum('skri,skoi->sro', flat_stack, flat_blocks, preferred_element_t...]
    reduce_sum x7 -> x0, other arithmetic: 17 us -> none  [dot_fields(): return jnp.sum(first * second, axis=(0, 1, 2, 3, 5))]
    convert_element_type x8 -> x0, other arithmetic: 14.5 us -> none  [operate(): rounded = field.astype(jnp.bfloat16)]
  transfers between devices with their start and end apart: 40 -> 0, of which waited for: 24 -> 0; matrix products, arithmetic and copies ran while one was open for 1% -> 0% of each run, Pallas kernels for 0% -> 0%
where the time goes in v1:
time: 276 us
  Pallas kernels  270 us (98%)
  local copies, waits for them, and re-layouts  5.22 us (2%)
    pallas_call x1, Pallas kernels, shards(): pl.pallas_call(functools.partial(kernel, n), out_shape=(field, field), in...  270 us

profile of v1, /device:TPU:0, one launch (start us, length us, event | category | flops | bytes accessed | tf_op | source)
XLA Modules:
  0.0 275.5 jit_solution(10050956045612326191)
XLA Ops:
  0.6 0.0 copy-start
  0.6 2.3 copy-done
  3.0 0.0 copy-start.1
  3.0 1.1 copy-done.1
  4.1 269.7 %shard_map.41 = (f32[16,96,128]{2,1,0:T(8,128)S(1)}, f32[16,96,128]{2,1,0:T(8,128)S(1)}) custom-call(f32[16,96,128]{2,1,0:T(8,128)S(1)} %bitcast.7, bf16[16,9,128,128]{3,2,1,0:T(8,128)(2,1)S(1)} %bitcast.4), custom_call_target="tpu_custom_call" | custom-call | tf_op jit(solution)/shard_map/pallas_call | solution.py:253
  273.8 0.9 copy.6
  274.7 0.9 copy.7
Async XLA Ops:
  0.6 2.3 copy-start
  3.0 1.1 copy-start.1

commit v2 on v1

--- a/solution.py
+++ b/solution.py
@@ -10,20 +10,21 @@
 CYCLES = 2
 KRYLOV = 4
 PARTS = 2
+SLOTS = 3
 UNROLL = 1
 
 mass_term = 3.5
 MESH = pl.DeviceIdType.MESH
 
 
-def dot_t(left, right):
+def dot(left, right):
     return lax.dot_general(
-        left, right, (((1,), (1,)), ((), ())), preferred_element_type=jnp.float32
+        left, right, (((1,), (0,)), ((), ())), preferred_element_type=jnp.float32
     )
 
 
 def kernel(
-    n, src, blocks, sol, res, w, halo, dirs, imgs, sbuf, rbuf,
+    n, src, blocks_in, sol, res, blocks, w, halo, dirs, imgs, sbuf, rbuf,
     halo_send, halo_recv, red_send, red_recv,
 ):
     sites, rhs, width = src.shape
@@ -87,11 +88,8 @@
     def to_column(row):
         return jnp.sum(jnp.where(eye, row, 0.0), axis=1, keepdims=True)
 
-    counter = [0]
-
-    def reduce_start(partials):
-        q = counter[0] % 2
-        counter[0] += 1
+    def reduce_start(p, slot, partials):
+        q = SLOTS * p + slot
         tile = jnp.zeros((8, 128), jnp.float32)
         for i, partial in enumerate(partials):
             tile = jnp.where(sub == i, to_row(partial), tile)
@@ -134,23 +132,24 @@
             k = 2 + 2 * bit - b if other else 1 + 2 * bit + b
             lefts.append(field_of(bit, mate))
             rights.append(blocks[s, k])
-        return dot_t(jnp.concatenate(lefts, axis=1), jnp.concatenate(rights, axis=1))
+        return dot(jnp.concatenate(lefts, axis=1), jnp.concatenate(rights, axis=0))
 
     def local_part(p, slot):
         def body(s, i, q, c):
             hops = hop_terms(s, i, q, lambda bit, m: w[p, m], False)
-            own = dot_t(w[p, s], blocks[s, 0])
+            own = dot(w[p, s], blocks[s, 0])
             imgs[slot, s, rs(p)] = mass_term * res[s, rs(p)] + own - hops
             return c
         over_sites(body, 0)
 
     zero = jnp.zeros((rows, width), jnp.float32)
 
-    def process(p, k, norms, last):
-        for copy in halo_copies(p):
-            copy.wait_recv()
-
-        def apply(s, i, q, c):
+    def process(k, norms, last):
+        groups = range(PARTS)
+        handles = [None] * PARTS
+        factors = [[] for _ in groups]
+
+        def apply(p, s, i, q, c):
             hops = hop_terms(s, i, q, lambda bit, m: halo[bit, p, m], True)
             image = imgs[k, s, rs(p)] - hops
             imgs[k, s, rs(p)] = image
@@ -158,62 +157,61 @@
                 return (c[0] + image * image, c[1] + image * res[s, rs(p)])
             return tuple(c[j] + image * imgs[j, s, rs(p)] for j in range(k))
 
-        sums = over_sites(apply, (zero,) * (k if k else 2))
-        if k:
-            total = reduce_end(reduce_start(sums))
-            factors = [to_column(total[j:j + 1] / norms[j]) for j in range(k)]
-
-            def orthogonal(s, i, q, c):
-                image = imgs[k, s, rs(p)]
-                for j in range(k):
-                    image = image - factors[j] * imgs[j, s, rs(p)]
-                imgs[k, s, rs(p)] = image
-                return (c[0] + image * image, c[1] + image * res[s, rs(p)])
-
-            sums = over_sites(orthogonal, (zero, zero))
-        handle = reduce_start(sums)
-
-        def steer(s, i, q, c):
+        def orthogonal(p, s, i, q, c):
+            image = imgs[k, s, rs(p)]
+            for j in range(k):
+                image = image - factors[p][j] * imgs[j, s, rs(p)]
+            imgs[k, s, rs(p)] = image
+            return (c[0] + image * image, c[1] + image * res[s, rs(p)])
+
+        def steer(p, s, i, q, c):
             direction = res[s, rs(p)]
             for j in range(k):
-                direction = direction - factors[j] * dirs[j, s, rs(p)]
+                direction = direction - factors[p][j] * dirs[j, s, rs(p)]
             dirs[k, s, rs(p)] = direction
             return c
 
-        over_sites(steer, 0)
-        for copy in halo_copies(p):
-            copy.wait_send()
-        total = reduce_end(handle)
-        norm = total[0:1]
-        alpha = to_column(total[1:2] / norm)
-
-        def shrink(s, i, q, c):
+        def shrink(p, alpha, s, i, q, c):
             residual = res[s, rs(p)] - alpha * imgs[k, s, rs(p)]
             res[s, rs(p)] = residual
             w[p, s] = residual.astype(jnp.bfloat16)
             return c
 
-        over_sites(shrink, 0)
-
-        def advance(s, i, q, c):
+        def advance(p, alpha, s, i, q, c):
             sol[s, rs(p)] = sol[s, rs(p)] + alpha * dirs[k, s, rs(p)]
             return c
 
-        def go_on():
-            start_halo(p)
-
-        def prepare():
-            local_part(p, (k + 1) % KRYLOV)
-
-        if last is None:
-            go_on()
-            over_sites(advance, 0)
-            prepare()
-        else:
-            pl.when(jnp.logical_not(last))(go_on)
-            over_sites(advance, 0)
-            pl.when(jnp.logical_not(last))(prepare)
-        return norms + [norm]
+        def when_going_on(body):
+            if last is None:
+                body()
+            else:
+                pl.when(jnp.logical_not(last))(body)
+
+        for p in groups:
+            for copy in halo_copies(p):
+                copy.wait_recv()
+            sums = over_sites(functools.partial(apply, p), (zero,) * (k if k else 2))
+            handles[p] = reduce_start(p, 0 if k else 2, sums)
+        if k:
+            for p in groups:
+                total = reduce_end(handles[p])
+                factors[p] = [to_column(total[j:j + 1] / norms[p][j]) for j in range(k)]
+                sums = over_sites(functools.partial(orthogonal, p), (zero, zero))
+                handles[p] = reduce_start(p, 1, sums)
+        for p in groups:
+            over_sites(functools.partial(steer, p), 0)
+        for p in groups:
+            for copy in halo_copies(p):
+                copy.wait_send()
+            total = reduce_end(handles[p])
+            norm = total[0:1]
+            norms[p].append(norm)
+            alpha = to_column(total[1:2] / norm)
+            over_sites(functools.partial(shrink, p, alpha), 0)
+            when_going_on(lambda p=p: start_halo(p))
+            over_sites(functools.partial(advance, p, alpha), 0)
+        for p in groups:
+            when_going_on(lambda p=p: local_part(p, (k + 1) % KRYLOV))
 
     def fill(s, i, q, c):
         value = src[s]
@@ -227,15 +225,21 @@
     pl.semaphore_wait(barrier, n - 1)
     for p in range(PARTS):
         start_halo(p)
+
+    def turn(s, i, q, c):
+        for k in range(blocks.shape[1]):
+            blocks[s, k] = blocks_in[s, k].T
+        return c
+
+    over_sites(turn, 0)
     for p in range(PARTS):
         local_part(p, 0)
 
     def cycle(index, c):
         norms = [[] for _ in range(PARTS)]
         for k in range(KRYLOV):
-            for p in range(PARTS):
-                last = index == CYCLES - 1 if k == KRYLOV - 1 else None
-                norms[p] = process(p, k, norms[p], last)
+            last = index == CYCLES - 1 if k == KRYLOV - 1 else None
+            process(k, norms, last)
         return c
 
     lax.fori_loop(0, CYCLES, cycle, 0)
@@ -256,16 +260,17 @@
         in_specs=[vmem, vmem],
         out_specs=(vmem, vmem),
         scratch_shapes=[
+            pltpu.VMEM((sites, count, width, width), jnp.bfloat16),
             pltpu.VMEM((PARTS, sites, rows, width), jnp.bfloat16),
             pltpu.VMEM((4, PARTS, sites, rows, width), jnp.bfloat16),
             pltpu.VMEM((KRYLOV, sites, rhs, width), jnp.float32),
             pltpu.VMEM((KRYLOV, sites, rhs, width), jnp.float32),
-            pltpu.VMEM((2, 8, 128), jnp.float32),
-            pltpu.VMEM((2, n - 1, 8, 128), jnp.float32),
+            pltpu.VMEM((SLOTS * PARTS, 8, 128), jnp.float32),
+            pltpu.VMEM((SLOTS * PARTS, n - 1, 8, 128), jnp.float32),
             pltpu.SemaphoreType.DMA((PARTS, 5)),
             pltpu.SemaphoreType.DMA((PARTS, 5)),
-            pltpu.SemaphoreType.DMA((2,)),
-            pltpu.SemaphoreType.DMA((2,)),
+            pltpu.SemaphoreType.DMA((SLOTS * PARTS,)),
+            pltpu.SemaphoreType.DMA((SLOTS * PARTS,)),
         ],
         compiler_params=pltpu.CompilerParams(
             collective_id=0, has_side_effects=True, vmem_limit_bytes=40 << 20

time: 276 us -> 232 us (0.84)
  Pallas kernels: 270 us -> 226 us
    pallas_call x1, Pallas kernels: 270 us -> 226 us  [shards(): pl.pallas_call(functools.partial(kernel, n), out_shape=(field, field), in...]
where the time goes in v2:
time: 232 us
  Pallas kernels  226 us (97%)
  local copies, waits for them, and re-layouts  5.22 us (2%)
    pallas_call x1, Pallas kernels, shards(): pl.pallas_call(functools.partial(kernel, n), out_shape=(field, field), in...  226 us
    unnamed x6, local copies, waits for them, and re-layouts  5.22 us

profile of v2, /device:TPU:0, one launch (start us, length us, event | category | flops | bytes accessed | tf_op | source)
XLA Modules:
  0.0 231.9 jit_solution(16653532797955733541)
XLA Ops:
  0.6 0.0 copy-start
  0.6 2.3 %copy-done = bf16[1,2,2,2,2,9,128,128]{7,6,5,4,3,2,1,0:T(8,128)(2,1)S(1)} copy-done((bf16[1,2,2,2,2,9,128,128]{7,6,5,4,3,2,1,0:T(8,128)(2,1)S(1)}, bf16[1,2,2,2,2,9,128,128]{7,6,5,4,3,2,1,0:T(8,128)(2,1)}, u32[]{:S(2)}) %copy-start) | copy-done | bytes 4718616
  3.0 0.0 copy-start.1
  3.0 1.1 copy-done.1
  4.1 226.0 %shard_map.41 = (f32[16,96,128]{2,1,0:T(8,128)S(1)}, f32[16,96,128]{2,1,0:T(8,128)S(1)}) custom-call(f32[16,96,128]{2,1,0:T(8,128)S(1)} %bitcast.7, bf16[16,9,128,128]{3,2,1,0:T(8,128)(2,1)S(1)} %bitcast.4), custom_call_target="tpu_custom_call" | custom-call | tf_op jit(solution)/shard_map/pallas_call | solution.py:257
  230.1 0.9 copy.6
  231.0 0.9 copy.7
Async XLA Ops:
  0.6 2.3 %copy-start = (bf16[1,2,2,2,2,9,128,128]{7,6,5,4,3,2,1,0:T(8,128)(2,1)S(1)}, bf16[1,2,2,2,2,9,128,128]{7,6,5,4,3,2,1,0:T(8,128)(2,1)}, u32[]{:S(2)}) copy-start(bf16[1,2,2,2,2,9,128,128]{7,6,5,4,3,2,1,0:T(8,128)(2,1)} %param.3) | copy-start | bytes 14155780
  3.0 1.1 copy-start.1

commit v3 on v2

--- a/solution.py
+++ b/solution.py
@@ -11,6 +11,7 @@
 KRYLOV = 4
 PARTS = 2
 SLOTS = 3
+SLAB = 4
 UNROLL = 1
 
 mass_term = 3.5
@@ -119,6 +120,11 @@
             return c
         return lax.fori_loop(0, sites // UNROLL, step, carry)
 
+    def over_slabs(body, carry):
+        def step(i, c):
+            return body(pl.ds(i * SLAB, SLAB), i, 0, c)
+        return lax.fori_loop(0, sites // SLAB, step, carry)
+
     def bit_of(i, q, bit):
         if (1 << bit) < UNROLL:
             return (q >> bit) & 1
@@ -162,7 +168,8 @@
             for j in range(k):
                 image = image - factors[p][j] * imgs[j, s, rs(p)]
             imgs[k, s, rs(p)] = image
-            return (c[0] + image * image, c[1] + image * res[s, rs(p)])
+            toward = image * res[s, rs(p)]
+            return (c[0] + jnp.sum(image * image, axis=0), c[1] + jnp.sum(toward, axis=0))
 
         def steer(p, s, i, q, c):
             direction = res[s, rs(p)]
@@ -196,10 +203,10 @@
             for p in groups:
                 total = reduce_end(handles[p])
                 factors[p] = [to_column(total[j:j + 1] / norms[p][j]) for j in range(k)]
-                sums = over_sites(functools.partial(orthogonal, p), (zero, zero))
+                sums = over_slabs(functools.partial(orthogonal, p), (zero, zero))
                 handles[p] = reduce_start(p, 1, sums)
         for p in groups:
-            over_sites(functools.partial(steer, p), 0)
+            over_slabs(functools.partial(steer, p), 0)
         for p in groups:
             for copy in halo_copies(p):
                 copy.wait_send()
@@ -207,9 +214,9 @@
             norm = total[0:1]
             norms[p].append(norm)
             alpha = to_column(total[1:2] / norm)
-            over_sites(functools.partial(shrink, p, alpha), 0)
+            over_slabs(functools.partial(shrink, p, alpha), 0)
             when_going_on(lambda p=p: start_halo(p))
-            over_sites(functools.partial(advance, p, alpha), 0)
+            over_slabs(functools.partial(advance, p, alpha), 0)
         for p in groups:
             when_going_on(lambda p=p: local_part(p, (k + 1) % KRYLOV))
 

time: 232 us -> 230 us (level)
  no operation moved by 1% of the time
where the time goes in v3:
time: 230 us
  Pallas kernels  224 us (97%)
  local copies, waits for them, and re-layouts  5.22 us (2%)
    pallas_call x1, Pallas kernels, shards(): pl.pallas_call(functools.partial(kernel, n), out_shape=(field, field), in...  224 us
    unnamed x6, local copies, waits for them, and re-layouts  5.22 us

profile of v3, /device:TPU:0, one launch (start us, length us, event | category | flops | bytes accessed | tf_op | source)
XLA Modules:
  0.0 230.1 jit_solution(13401550720946950113)
XLA Ops:
  0.6 0.0 copy-start
  0.6 2.3 %copy-done = bf16[1,2,2,2,2,9,128,128]{7,6,5,4,3,2,1,0:T(8,128)(2,1)S(1)} copy-done((bf16[1,2,2,2,2,9,128,128]{7,6,5,4,3,2,1,0:T(8,128)(2,1)S(1)}, bf16[1,2,2,2,2,9,128,128]{7,6,5,4,3,2,1,0:T(8,128)(2,1)}, u32[]{:S(2)}) %copy-start) | copy-done | bytes 4718616
  3.0 0.0 copy-start.1
  3.0 1.1 copy-done.1
  4.1 224.3 %shard_map.41 = (f32[16,96,128]{2,1,0:T(8,128)S(1)}, f32[16,96,128]{2,1,0:T(8,128)S(1)}) custom-call(f32[16,96,128]{2,1,0:T(8,128)S(1)} %bitcast.7, bf16[16,9,128,128]{3,2,1,0:T(8,128)(2,1)S(1)} %bitcast.4), custom_call_target="tpu_custom_call" | custom-call | tf_op jit(solution)/shard_map/pallas_call | solution.py:264
  228.4 0.9 copy.6
  229.2 0.9 copy.7
Async XLA Ops:
  0.6 2.3 %copy-start = (bf16[1,2,2,2,2,9,128,128]{7,6,5,4,3,2,1,0:T(8,128)(2,1)S(1)}, bf16[1,2,2,2,2,9,128,128]{7,6,5,4,3,2,1,0:T(8,128)(2,1)}, u32[]{:S(2)}) copy-start(bf16[1,2,2,2,2,9,128,128]{7,6,5,4,3,2,1,0:T(8,128)(2,1)} %param.3) | copy-start | bytes 14155780
  3.0 1.1 copy-start.1
